TPU v7x, 32 devices: a whole 2x2x4 slice. The times are simulated.
32 devices in a mesh: tm: 4 (over y, x), space: 8 (over z, core).
Axes of the slice: x: 2, y: 2, z: 4, core: 2. Of those that a mesh axis runs over, the one named last changes fastest.
Arguments:
- latent_clip: bfloat16 [8, 16, 32, 256], P('tm', 'space'), may hold values from -45 to 45
- cotangent: bfloat16 [8, 16, 32, 128], P('tm', 'space'), may hold values from -6 to 6
- conv_weight: bfloat16 [6912, 128], replicated, may hold values from -0.078125 to 0.078125
- norm_gain: float32 [256], replicated, may hold values from 0.5 to 1.5
- norm_shift: float32 [256], replicated, may hold values from -2 to 2
Outputs:
- clip_grad: bfloat16 [8, 16, 32, 256], P('tm', 'space')
- weight_grad: float32 [6912, 128], P('space')
- gain_grad: float32 [256], replicated
- shift_grad: float32 [256], replicated
All inputs are finite; a program needn't handle non-finite values.
Results may differ from a plain program's by a relative error of at most 0.0029.
Values may be sent and summed in bfloat16 or wider, within the bound.
A program may use at most 64 MiB of HBM per device.

v0:
```python
import jax
import jax.numpy as jnp
from jax import lax
from jax.sharding import PartitionSpec as P

GROUPS = 32


def shifted(value, axis, steps):
    count = lax.axis_size(axis)
    leading, last = (max(0, -steps), min(count, count - steps))
    return lax.ppermute(value, axis, [(source, source + steps) for source in range(leading, last)])


def extended_2(block, sides, width):
    for axis, dim in sides:
        count = lax.axis_size(axis)
        forward = [(i, i + 1) for i in range(count - 1)]
        backward = [(target, source) for source, target in forward]
        low = lax.ppermute(
            lax.slice_in_dim(block, block.shape[dim] - width, None, axis=dim), axis, forward
        )
        high = lax.ppermute(lax.slice_in_dim(block, 0, width, axis=dim), axis, backward)
        block = jnp.concatenate([low, block, high], axis=dim)
    return block


def silu_slope(activation):
    sigma = jax.nn.sigmoid(activation)
    return sigma * (1.0 + activation * (1.0 - sigma))


def tap_block(source, anchors, frame_count, row_count, col_count):
    pieces = [
        source[
            anchor[0] : anchor[0] + frame_count,
            anchor[1] : anchor[1] + row_count,
            anchor[2] : anchor[2] + col_count,
            :,
        ]
        for anchor in anchors
    ]
    merged = jnp.concatenate(pieces, axis=-1)
    return merged.reshape(frame_count * row_count * col_count, merged.shape[-1])


def transposed(grad_pad, conv_weight, frame_count, row_count, col_count):
    out_channels = conv_weight.shape[1]
    channels = conv_weight.shape[0] // 27
    kernel = conv_weight.reshape(3, 3, 3, channels, out_channels)
    total = jnp.zeros((frame_count * row_count * col_count, channels), jnp.float32)
    for tap_time in range(3):
        anchors = [
            (2 - tap_time, 2 - tap_row, 2 - tap_col) for tap_row in range(3) for tap_col in range(3)
        ]
        tap_cols = tap_block(grad_pad, anchors, frame_count, row_count, col_count)
        flipped = jnp.transpose(kernel[tap_time], (0, 1, 3, 2)).reshape(9 * out_channels, channels)
        total = total + jnp.dot(tap_cols, flipped, preferred_element_type=jnp.float32)
    return total.reshape(frame_count, row_count, col_count, channels)


def shards(latent_clip, cotangent, conv_weight, norm_gain, norm_shift):
    frame_count, row_count, col_count, channels = latent_clip.shape
    out_channels = cotangent.shape[-1]
    width_group = channels // GROUPS
    tm_size = lax.axis_size("tm")
    space_size = lax.axis_size("space")
    group_count = frame_count * row_count * col_count * width_group * tm_size * space_size
    values = latent_clip.astype(jnp.float32).reshape(
        frame_count, row_count, col_count, GROUPS, width_group
    )
    group_mean = lax.psum(jnp.sum(values, axis=(0, 1, 2, 4)), ("tm", "space")) / group_count
    centered = values - group_mean[:, None]
    group_var = (
        lax.psum(jnp.sum(centered * centered, axis=(0, 1, 2, 4)), ("tm", "space")) / group_count
    )
    inv_std = lax.rsqrt(group_var + 1e-06)
    normed = (centered * inv_std[:, None]).reshape(frame_count, row_count, col_count, channels)
    activation = normed * norm_gain + norm_shift
    hidden = jax.nn.silu(activation).astype(jnp.bfloat16)
    ahead = shifted(cotangent, "tm", -1)
    time_source = jnp.concatenate([cotangent, ahead], axis=0)
    time_pad = (0, 0)
    cached = shifted(hidden, "tm", 1)
    extended = jnp.concatenate([cached, hidden], axis=0)
    rimmed = extended_2(extended, (("space", 1),), 1)
    padded = jnp.pad(rimmed, ((0, 0), (0, 0), (1, 1), (0, 0)))
    cell_count = frame_count * row_count * col_count
    upstream = cotangent.reshape(cell_count, out_channels)
    tap_grads = []
    for tap_time in range(3):
        anchors = [(tap_time, tap_row, tap_col) for tap_row in range(3) for tap_col in range(3)]
        tap_cols = tap_block(padded, anchors, frame_count, row_count, col_count)
        tap_grads.append(
            lax.dot_general(
                tap_cols, upstream, (((0,), (0,)), ((), ())), preferred_element_type=jnp.float32
            )
        )
    local_grad = jnp.concatenate(tap_grads, axis=0)
    space_shard = lax.psum_scatter(local_grad, "space", scatter_dimension=0, tiled=True)
    weight_grad = lax.psum(space_shard, "tm")
    grad_pad = jnp.pad(time_source, (time_pad, (2, 2), (1, 1), (0, 0)))
    spread = transposed(grad_pad, conv_weight, frame_count, row_count + 2, col_count)
    from_below = shifted(spread[:, 0], "space", -1)
    from_above = shifted(spread[:, row_count + 1], "space", 1)
    inner = spread[:, 1 : row_count + 1]
    inner = inner.at[:, row_count - 1].add(from_below)
    inner = inner.at[:, 0].add(from_above)
    activation_grad = inner * silu_slope(activation)
    gain_grad, shift_grad = lax.psum(
        (
            jnp.sum(activation_grad * normed, axis=(0, 1, 2)),
            jnp.sum(activation_grad, axis=(0, 1, 2)),
        ),
        ("tm", "space"),
    )
    first = jnp.sum((norm_gain * shift_grad).reshape(GROUPS, width_group), axis=1)
    second = jnp.sum((norm_gain * gain_grad).reshape(GROUPS, width_group), axis=1)
    scaled = (activation_grad * norm_gain).reshape(
        frame_count, row_count, col_count, GROUPS, width_group
    )
    normed_groups = normed.reshape(frame_count, row_count, col_count, GROUPS, width_group)
    clip_grad = inv_std[:, None] * (
        scaled - first[:, None] / group_count - normed_groups * second[:, None] / group_count
    )
    clip_grad = clip_grad.reshape(frame_count, row_count, col_count, channels).astype(jnp.bfloat16)
    return (clip_grad, weight_grad, gain_grad, shift_grad)


def solution(mesh):
    return jax.shard_map(
        shards,
        mesh=mesh,
        in_specs=(P("tm", "space", None, None), P("tm", "space", None, None), P(), P(), P()),
        out_specs=(P("tm", "space", None, None), P("space", None), P(), P()),
        check_vma=False,
    )
```

profile of v0, /device:TPU:0, one launch (start us, length us, event | category | flops | bytes accessed | tf_op | source)
XLA Modules:
  0.0 225.5 jit_solution(13261450040164895884)
XLA Ops:
  7.2 0.0 reduce-scatter.2.cloned.1.call-start
  7.2 0.9 convert_reduce_fusion
  8.1 0.1 reduce_sum.69
  8.2 0.1 reduce_sum.70
  8.3 1.3 collective-permute-start
  9.6 43.2 %psum.35 = f32[32]{0:T(128)S(1)} all-reduce(f32[32]{0:T(128)S(1)} %reduce_sum.70), channel_id=1, replica_groups=mesh['tm'=4,'space'=8] {'tm','space'}, use_global_device_ids=true, to_apply=%region_2.0 | all-reduce | flops 32 | bytes 256 | tf_op jit(solution)/shard_map/psum | solution.py:72
  52.8 0.1 sub.35
  52.8 0.1 sub.36
  52.9 0.9 fusion.33
  53.8 0.1 reduce_sum.72
  53.9 0.1 reduce_sum.73
  54.0 1.5 fusion.40
  55.6 41.0 %psum.36 = f32[32]{0:T(128)S(1)} all-reduce(f32[32]{0:T(128)S(1)} %reduce_sum.73), channel_id=1, replica_groups=mesh['tm'=4,'space'=8] {'tm','space'}, use_global_device_ids=true, to_apply=%region_5.6 | all-reduce | flops 32 | bytes 256 | tf_op jit(solution)/shard_map/psum | solution.py:75
  96.6 0.2 copy.15
  96.8 0.0 copy-start.1
  96.8 0.2 copy.13
  97.1 0.2 copy.14
  97.3 0.2 copy-done.1
  97.7 0.1 constant_dynamic-update-slice_fusion.25
  97.7 0.1 constant_dynamic-update-slice_fusion.24
  97.8 0.1 constant_dynamic-update-slice_fusion.23
  97.9 0.1 constant_dynamic-update-slice_fusion.22
  98.0 0.1 constant_dynamic-update-slice_fusion.21
  98.0 0.1 constant_dynamic-update-slice_fusion.20
  98.1 0.1 constant_dynamic-update-slice_fusion.19
  98.2 0.1 constant_dynamic-update-slice_fusion.18
  98.3 0.3 fusion.42
  98.6 0.3 convolution_add_fusion.1
  99.0 0.0 copy-start
  99.0 0.0 copy-start.2
  99.0 0.0 copy-start.3
  99.0 0.3 convolution_add_fusion
  99.4 1.3 collective-permute-start.1
  100.7 0.1 mul.75
  100.8 0.1 mul.76
  100.9 3.0 %collective-permute-start.2 = (f32[2,32,256]{2,1,0:T(8,128)S(1)}, f32[2,32,256]{2,1,0:T(8,128)S(1)}, u32[]{:S(2)}, u32[]{:S(2)}) collective-permute-start(f32[2,32,256]{2,1,0:T(8,128)S(1)} %get-tuple-element.53), channel_id=1, source_target_pairs={{0,1},{1,2},{2,3},{3,4},{4,5},{5,6},{6,7},{8,9},{9,10},{10,11},{11... | collective-permute-start | bytes 196616 | tf_op jit(solution)/shard_map/ppermute | solution.py:12
  103.9 0.9 collective-permute-done.2
  104.8 0.1 fusion.38
  105.0 4.2 %collective-permute-start.3 = (bf16[2,2,32,256]{3,2,1,0:T(8,128)(2,1)S(1)}, bf16[2,2,32,256]{3,2,1,0:T(8,128)(2,1)S(1)}, u32[]{:S(2)}, u32[]{:S(2)}) collective-permute-start(bf16[2,2,32,256]{3,2,1,0:T(8,128)(2,1)S(1)} %get-tuple-element.90), channel_id=1, source_target_pairs={{0,8},{8,16},{16,24},{1,9},{9,17},{17,25},{2,10},{10,18},{18,26},{... | collective-permute-start | bytes 196616 | tf_op jit(solution)/shard_map/ppermute | solution.py:12
  109.1 1.9 collective-permute-done.3
  111.1 1.4 collective-permute-start.4
  112.6 1.3 collective-permute-start.5
  113.9 4.6 %collective-permute-done.5 = bf16[4,1,32,256]{3,2,1,0:T(8,128)(2,1)S(1)} collective-permute-done((bf16[4,1,32,256]{3,2,1,0:T(8,128)(2,1)S(1)}, bf16[4,1,32,256]{3,2,1,0:T(8,128)(2,1)S(1)}, u32[]{:S(2)}, u32[]{:S(2)}) %collective-permute-start.5) | collective-permute-done | bytes 65568 | tf_op jit(solution)/shard_map/ppermute | solution.py:23
  118.4 0.1 select_maximum_fusion
  118.9 0.3 convolution_bitcast_fusion
  119.2 0.3 convolution_bitcast_fusion.2
  119.6 0.3 convolution_bitcast_fusion.1
  119.9 2.0 pad_maximum_fusion
  121.9 0.0 reduce-scatter.2.cloned.1.call-update
  122.0 0.0 all-reduce.5.cloned.1.call-start
  122.0 45.1 %all-reduce.2 = (f32[256]{0:T(256)S(1)}, f32[256]{0:T(256)S(1)}) all-reduce(f32[256]{0:T(256)S(1)} %get-tuple-element.29, f32[256]{0:T(256)S(1)} %get-tuple-element.28), channel_id=1, replica_groups=mesh['tm'=4,'space'=8] {'tm','space'}, use_global_device_ids=true, to_apply=%region_10.11 | all-reduce | flops 512 | bytes 4096 | tf_op jit(solution)/shard_map/psum | solution.py:110
  167.2 0.1 reshape.151
  167.2 0.1 reduce_sum.75
  167.4 3.1 %reduce-scatter.2.cloned.1.call-done = f32[864,128]{1,0:T(8,128)} async-done(((f32[6912,128]{1,0:T(8,128)}), f32[864,128]{1,0:T(8,128)}) %reduce-scatter.2.cloned.1.call-update) | async-done | bytes 442384 | tf_op jit(solution)/shard_map/reduce_scatter | solution.py:100
  170.5 0.0 all-reduce.5.cloned.1.call-update
  170.5 0.1 sub.40
  170.6 0.1 sub.41
  170.7 0.1 reshape.152
  170.8 0.1 reduce_sum.77
  170.9 0.1 mul.88
  171.0 0.1 mul.89
  171.1 0.7 fusion.32
  171.8 45.1 %all-reduce.5.cloned.1.call-done = f32[864,128]{1,0:T(8,128)} async-done(((f32[864,128]{1,0:T(8,128)}), f32[864,128]{1,0:T(8,128)}) %all-reduce.5.cloned.1.call-update) | async-done | bytes 442384 | tf_op jit(solution)/shard_map/psum | solution.py:101
  216.9 1.8 copy.74
  (35 shorter events, 0.4 us)
Async XLA Ops:
  7.2 163.3 %reduce-scatter.2.cloned.1.call-start = ((), (), s32[]{:S(2)}) async-start(), calls=%async_computation.1 | async-start | bytes 3981312 | tf_op jit(solution)/shard_map/reduce_scatter | solution.py:100
  8.3 89.0 %collective-permute-start = (bf16[2,2,32,128]{3,2,1,0:T(8,128)(2,1)}, bf16[2,2,32,128]{3,2,1,0:T(8,128)(2,1)S(1)}, u32[]{:S(2)}, u32[]{:S(2)}) collective-permute-start(bf16[2,2,32,128]{3,2,1,0:T(8,128)(2,1)} %param.10), channel_id=1, source_target_pairs={{8,0},{16,8},{24,16},{9,1},{17,9},{25,17},{10,2},{18,10},{26,18},{... | collective-permute-start | bytes 98312 | tf_op jit(solution)/shard_map/ppermute | solution.py:12
  96.8 0.8 copy-start.1
  99.0 5.8 %copy-start = (bf16[2,2,32,256]{3,2,1,0:T(8,128)(2,1)S(1)}, bf16[2,2,32,256]{3,2,1,0:T(8,128)(2,1)}, u32[]{:S(2)}) copy-start(bf16[2,2,32,256]{3,2,1,0:T(8,128)(2,1)} %param.9) | copy-start | bytes 196612
  99.0 5.8 %copy-start.2 = (f32[256]{0:T(256)S(1)}, f32[256]{0:T(256)}, u32[]{:S(2)}) copy-start(f32[256]{0:T(256)} %param.12) | copy-start | bytes 3076
  99.0 5.8 %copy-start.3 = (f32[256]{0:T(256)S(1)}, f32[256]{0:T(256)}, u32[]{:S(2)}) copy-start(f32[256]{0:T(256)} %param.13) | copy-start | bytes 3076
  99.4 4.5 %collective-permute-start.1 = (f32[2,32,256]{2,1,0:T(8,128)S(1)}, f32[2,32,256]{2,1,0:T(8,128)S(1)}, u32[]{:S(2)}, u32[]{:S(2)}) collective-permute-start(f32[2,32,256]{2,1,0:T(8,128)S(1)} %get-tuple-element.54), channel_id=1, source_target_pairs={{1,0},{2,1},{3,2},{4,3},{5,4},{6,5},{7,6},{9,8},{10,9},{11,10},{12... | collective-permute-start | bytes 196616 | tf_op jit(solution)/shard_map/ppermute | solution.py:12
  100.9 3.9 %collective-permute-start.2 = (f32[2,32,256]{2,1,0:T(8,128)S(1)}, f32[2,32,256]{2,1,0:T(8,128)S(1)}, u32[]{:S(2)}, u32[]{:S(2)}) collective-permute-start(f32[2,32,256]{2,1,0:T(8,128)S(1)} %get-tuple-element.53), channel_id=1, source_target_pairs={{0,1},{1,2},{2,3},{3,4},{4,5},{5,6},{6,7},{8,9},{9,10},{10,11},{11... | collective-permute-start | bytes 196616 | tf_op jit(solution)/shard_map/ppermute | solution.py:12
  105.0 6.1 %collective-permute-start.3 = (bf16[2,2,32,256]{3,2,1,0:T(8,128)(2,1)S(1)}, bf16[2,2,32,256]{3,2,1,0:T(8,128)(2,1)S(1)}, u32[]{:S(2)}, u32[]{:S(2)}) collective-permute-start(bf16[2,2,32,256]{3,2,1,0:T(8,128)(2,1)S(1)} %get-tuple-element.90), channel_id=1, source_target_pairs={{0,8},{8,16},{16,24},{1,9},{9,17},{17,25},{2,10},{10,18},{18,26},{... | collective-permute-start | bytes 196616 | tf_op jit(solution)/shard_map/ppermute | solution.py:12
  111.1 2.8 %collective-permute-start.4 = (bf16[4,1,32,256]{3,2,1,0:T(8,128)(2,1)S(1)}, bf16[4,1,32,256]{3,2,1,0:T(8,128)(2,1)S(1)}, u32[]{:S(2)}, u32[]{:S(2)}) collective-permute-start(bf16[4,1,32,256]{3,2,1,0:T(8,128)(2,1)S(1)} %get-tuple-element.88), channel_id=1, source_target_pairs={{0,1},{1,2},{2,3},{3,4},{4,5},{5,6},{6,7},{8,9},{9,10},{10,11},{11... | collective-permute-start | bytes 196616 | tf_op jit(solution)/shard_map/ppermute | solution.py:20
  112.6 5.9 %collective-permute-start.5 = (bf16[4,1,32,256]{3,2,1,0:T(8,128)(2,1)S(1)}, bf16[4,1,32,256]{3,2,1,0:T(8,128)(2,1)S(1)}, u32[]{:S(2)}, u32[]{:S(2)}) collective-permute-start(bf16[4,1,32,256]{3,2,1,0:T(8,128)(2,1)S(1)} %get-tuple-element.89), channel_id=1, source_target_pairs={{1,0},{2,1},{3,2},{4,3},{5,4},{6,5},{7,6},{9,8},{10,9},{11,10},{12... | collective-permute-start | bytes 196616 | tf_op jit(solution)/shard_map/ppermute | solution.py:23
  122.0 94.9 %all-reduce.5.cloned.1.call-start = ((), (), s32[]{:S(2)}) async-start(), calls=%async_computation.2 | async-start | bytes 884736 | tf_op jit(solution)/shard_map/psum | solution.py:101
  167.2 51.5 %copy-start.4 = (f32[256]{0:T(256)}, f32[256]{0:T(256)S(1)}, u32[]{:S(2)}) copy-start(f32[256]{0:T(256)S(1)} %get-tuple-element.97) | copy-start | bytes 3076
  167.2 51.5 %copy-start.5 = (f32[256]{0:T(256)}, f32[256]{0:T(256)S(1)}, u32[]{:S(2)}) copy-start(f32[256]{0:T(256)S(1)} %get-tuple-element.98) | copy-start | bytes 3076
Sparse Core Ops, SparseCore 0:
  122.1 48.3 reduce-scatter.1
  173.8 43.0 all-reduce.4
where the time goes:
time: 226 us
  blocking collectives  129 us (57%)
  waiting for transfers between devices  55.6 us (25%)
  between operations  14.5 us (6%)
  starting transfers between devices  12.6 us (6%)
  local copies, waits for them, and re-layouts  6.15 us (3%)
  other arithmetic  5.25 us (2%)
    psum x1, blocking collectives, shards(): lax.psum((jnp.sum(activation_grad * normed, axis=(0, 1, 2)), jnp.sum(acti...  45.1 us
    psum x1, waiting for transfers between devices, shards(): weight_grad = lax.psum(space_shard, 'tm')  45.1 us
    psum x1, blocking collectives, shards(): lax.psum(jnp.sum(values, axis=(0, 1, 2, 4)), ('tm', 'space')) / group_count  43.2 us
    psum x1, blocking collectives, shards(): lax.psum(jnp.sum(centered * centered, axis=(0, 1, 2, 4)), ('tm', 'space'))  41 us
    ppermute x4, starting transfers between devices, shifted(): lax.ppermute(value, axis, [(source, source + steps) for source in range(l...  9.8 us
    ppermute x1, waiting for transfers between devices, extended_2(): lax.ppermute(lax.slice_in_dim(block, 0, width, axis=dim), axis, backward)  4.55 us
  transfers between devices with their start and end apart: 8, of which 5 were waited for; matrix products, arithmetic and copies ran while one was open for 2% of the time, Pallas kernels for 0%

commit v1 on v0

--- a/solution.py
+++ b/solution.py
@@ -1,9 +1,19 @@
+import functools
 import jax
 import jax.numpy as jnp
 from jax import lax
 from jax.sharding import PartitionSpec as P
 
 GROUPS = 32
+
+
+def prepare_lane_in(inputs, bus_axis, named_axis):
+    for h in (bus_axis, named_axis):
+        inputs = lax.psum(inputs, h)
+    return inputs
+
+
+kinds_order = functools.partial(prepare_lane_in, bus_axis="space", named_axis="tm")
 
 
 def shifted(value, axis, steps):
@@ -71,9 +81,7 @@
     )
     group_mean = lax.psum(jnp.sum(values, axis=(0, 1, 2, 4)), ("tm", "space")) / group_count
     centered = values - group_mean[:, None]
-    group_var = (
-        lax.psum(jnp.sum(centered * centered, axis=(0, 1, 2, 4)), ("tm", "space")) / group_count
-    )
+    group_var = kinds_order(jnp.sum(centered * centered, axis=(0, 1, 2, 4))) / group_count
     inv_std = lax.rsqrt(group_var + 1e-06)
     normed = (centered * inv_std[:, None]).reshape(frame_count, row_count, col_count, channels)
     activation = normed * norm_gain + norm_shift

time: 226 us -> 205 us (0.907)
  blocking collectives: 129 us -> 112 us
    psum x1 -> x2, blocking collectives: 41 us -> 24.1 us  [prepare_lane_in(): inputs = lax.psum(inputs, h)]
where the time goes in v1:
time: 205 us
  blocking collectives  112 us (55%)
  waiting for transfers between devices  55.5 us (27%)
  between operations  14.5 us (7%)
  starting transfers between devices  10.9 us (5%)
  local copies, waits for them, and re-layouts  5.95 us (3%)
  other arithmetic  4.4 us (2%)
  matrix products  2.07 us (1%)
    psum x1, waiting for transfers between devices, shards(): weight_grad = lax.psum(space_shard, 'tm')  45.1 us
    psum x1, blocking collectives, shards(): lax.psum((jnp.sum(activation_grad * normed, axis=(0, 1, 2)), jnp.sum(acti...  44.3 us
    psum x1, blocking collectives, shards(): lax.psum(jnp.sum(values, axis=(0, 1, 2, 4)), ('tm', 'space')) / group_count  43.2 us
    psum x2, blocking collectives, prepare_lane_in(): inputs = lax.psum(inputs, h)  24.1 us
    ppermute x4, starting transfers between devices, shifted(): lax.ppermute(value, axis, [(source, source + steps) for source in range(l...  8.06 us
    ppermute x1, waiting for transfers between devices, extended_2(): lax.ppermute(lax.slice_in_dim(block, 0, width, axis=dim), axis, backward)  4.55 us
  transfers between devices with their start and end apart: 8, of which 5 were waited for; matrix products, arithmetic and copies ran while one was open for 2% of the time, Pallas kernels for 0%

profile of v1, /device:TPU:0, one launch (start us, length us, event | category | flops | bytes accessed | tf_op | source)
XLA Modules:
  0.0 204.8 jit_solution(4642453897287166985)
XLA Ops:
  7.2 0.0 reduce-scatter.2.cloned.1.call-start
  7.2 0.9 convert_reduce_fusion
  8.1 0.1 reduce_sum.69
  8.2 0.1 reduce_sum.70
  8.3 1.3 collective-permute-start
  9.6 43.2 %psum.42 = f32[32]{0:T(128)S(1)} all-reduce(f32[32]{0:T(128)S(1)} %reduce_sum.70), channel_id=1, replica_groups=mesh['tm'=4,'space'=8] {'tm','space'}, use_global_device_ids=true, to_apply=%region_2.0 | all-reduce | flops 32 | bytes 256 | tf_op jit(solution)/shard_map/psum | solution.py:82
  52.8 0.1 sub.35
  52.8 0.1 sub.36
  52.9 0.0 copy-start
  52.9 1.6 fusion.40
  54.6 0.1 reduce_sum.72
  54.6 0.1 reduce_sum.73
  54.8 0.3 copy.15
  55.0 0.0 copy-start.1
  55.0 0.2 copy.13
  55.3 0.2 copy.14
  55.5 14.4 %psum.43 = f32[32]{0:T(128)S(1)} all-reduce(f32[32]{0:T(128)S(1)} %reduce_sum.73), channel_id=1, replica_groups=mesh['tm'=4,'space'=8] {'space'}, use_global_device_ids=true, to_apply=%region_5.6 | all-reduce | flops 32 | bytes 256 | tf_op jit(solution)/shard_map/psum | solution.py:12
  70.0 9.7 %psum.44 = f32[32]{0:T(128)S(1)} all-reduce(f32[32]{0:T(128)S(1)} %psum.43), channel_id=1, replica_groups=mesh['tm'=4,'space'=8] {'tm'}, use_global_device_ids=true, to_apply=%region_6.7 | all-reduce | flops 32 | bytes 256 | tf_op jit(solution)/shard_map/psum | solution.py:12
  79.8 0.1 constant_dynamic-update-slice_fusion.25
  79.9 0.1 constant_dynamic-update-slice_fusion.24
  79.9 0.1 constant_dynamic-update-slice_fusion.23
  80.0 0.1 constant_dynamic-update-slice_fusion.22
  80.1 0.1 constant_dynamic-update-slice_fusion.21
  80.1 0.1 constant_dynamic-update-slice_fusion.20
  80.2 0.1 constant_dynamic-update-slice_fusion.19
  80.3 0.1 constant_dynamic-update-slice_fusion.18
  80.4 0.3 fusion.42
  80.7 0.3 convolution_add_fusion.1
  81.1 0.0 copy-start.2
  81.1 0.0 copy-start.3
  81.1 0.3 convolution_add_fusion
  81.5 1.3 collective-permute-start.1
  82.8 0.1 mul.75
  82.9 0.1 mul.76
  83.0 3.0 %collective-permute-start.2 = (f32[2,32,256]{2,1,0:T(8,128)S(1)}, f32[2,32,256]{2,1,0:T(8,128)S(1)}, u32[]{:S(2)}, u32[]{:S(2)}) collective-permute-start(f32[2,32,256]{2,1,0:T(8,128)S(1)} %get-tuple-element.53), channel_id=1, source_target_pairs={{0,1},{1,2},{2,3},{3,4},{4,5},{5,6},{6,7},{8,9},{9,10},{10,11},{11... | collective-permute-start | bytes 196616 | tf_op jit(solution)/shard_map/ppermute | solution.py:22
  86.0 0.0 collective-permute-done.1
  86.0 0.9 collective-permute-done.2
  86.9 0.1 fusion.38
  87.0 2.4 %collective-permute-start.3 = (bf16[2,2,32,256]{3,2,1,0:T(8,128)(2,1)S(1)}, bf16[2,2,32,256]{3,2,1,0:T(8,128)(2,1)S(1)}, u32[]{:S(2)}, u32[]{:S(2)}) collective-permute-start(bf16[2,2,32,256]{3,2,1,0:T(8,128)(2,1)S(1)} %get-tuple-element.90), channel_id=1, source_target_pairs={{0,8},{8,16},{16,24},{1,9},{9,17},{17,25},{2,10},{10,18},{18,26},{... | collective-permute-start | bytes 196616 | tf_op jit(solution)/shard_map/ppermute | solution.py:22
  89.5 1.9 collective-permute-done.3
  91.4 1.4 collective-permute-start.4
  92.9 1.3 collective-permute-start.5
  94.2 4.6 %collective-permute-done.5 = bf16[4,1,32,256]{3,2,1,0:T(8,128)(2,1)S(1)} collective-permute-done((bf16[4,1,32,256]{3,2,1,0:T(8,128)(2,1)S(1)}, bf16[4,1,32,256]{3,2,1,0:T(8,128)(2,1)S(1)}, u32[]{:S(2)}, u32[]{:S(2)}) %collective-permute-start.5) | collective-permute-done | bytes 65568 | tf_op jit(solution)/shard_map/ppermute | solution.py:33
  98.8 0.1 select_maximum_fusion
  99.2 0.3 convolution_bitcast_fusion
  99.6 0.3 convolution_bitcast_fusion.2
  99.9 0.3 convolution_bitcast_fusion.1
  100.3 2.0 pad_maximum_fusion
  102.3 0.0 reduce-scatter.2.cloned.1.call-update
  102.3 0.0 all-reduce.5.cloned.1.call-start
  102.3 44.3 %all-reduce.2 = (f32[256]{0:T(256)S(1)}, f32[256]{0:T(256)S(1)}) all-reduce(f32[256]{0:T(256)S(1)} %get-tuple-element.29, f32[256]{0:T(256)S(1)} %get-tuple-element.28), channel_id=1, replica_groups=mesh['tm'=4,'space'=8] {'tm','space'}, use_global_device_ids=true, to_apply=%region_11.12 | all-reduce | flops 512 | bytes 4096 | tf_op jit(solution)/shard_map/psum | solution.py:118
  146.6 0.1 reshape.151
  146.7 0.1 reduce_sum.75
  146.8 3.0 %reduce-scatter.2.cloned.1.call-done = f32[864,128]{1,0:T(8,128)} async-done(((f32[6912,128]{1,0:T(8,128)}), f32[864,128]{1,0:T(8,128)}) %reduce-scatter.2.cloned.1.call-update) | async-done | bytes 442384 | tf_op jit(solution)/shard_map/reduce_scatter | solution.py:108
  149.8 0.0 all-reduce.5.cloned.1.call-update
  149.9 0.1 sub.40
  149.9 0.1 sub.41
  150.0 0.1 reshape.152
  150.1 0.1 reduce_sum.77
  150.2 0.1 mul.88
  150.3 0.1 mul.89
  150.4 0.7 fusion.32
  151.1 45.1 %all-reduce.5.cloned.1.call-done = f32[864,128]{1,0:T(8,128)} async-done(((f32[864,128]{1,0:T(8,128)}), f32[864,128]{1,0:T(8,128)}) %all-reduce.5.cloned.1.call-update) | async-done | bytes 442384 | tf_op jit(solution)/shard_map/psum | solution.py:109
  196.2 1.8 copy.74
  (36 shorter events, 0.5 us)
Async XLA Ops:
  7.2 142.7 %reduce-scatter.2.cloned.1.call-start = ((), (), s32[]{:S(2)}) async-start(), calls=%async_computation.1 | async-start | bytes 3981312 | tf_op jit(solution)/shard_map/reduce_scatter | solution.py:108
  8.3 71.4 %collective-permute-start = (bf16[2,2,32,128]{3,2,1,0:T(8,128)(2,1)}, bf16[2,2,32,128]{3,2,1,0:T(8,128)(2,1)S(1)}, u32[]{:S(2)}, u32[]{:S(2)}) collective-permute-start(bf16[2,2,32,128]{3,2,1,0:T(8,128)(2,1)} %param.10), channel_id=1, source_target_pairs={{8,0},{16,8},{24,16},{9,1},{17,9},{25,17},{10,2},{18,10},{26,18},{... | collective-permute-start | bytes 98312 | tf_op jit(solution)/shard_map/ppermute | solution.py:22
  52.9 1.6 copy-start
  55.0 24.7 %copy-start.1 = (bf16[2,2,32,128]{3,2,1,0:T(8,128)(2,1)S(1)}, bf16[2,2,32,128]{3,2,1,0:T(8,128)(2,1)}, u32[]{:S(2)}) copy-start(bf16[2,2,32,128]{3,2,1,0:T(8,128)(2,1)} %param.10) | copy-start | bytes 98308
  81.1 5.8 %copy-start.2 = (f32[256]{0:T(256)S(1)}, f32[256]{0:T(256)}, u32[]{:S(2)}) copy-start(f32[256]{0:T(256)} %param.12) | copy-start | bytes 3076
  81.1 5.8 %copy-start.3 = (f32[256]{0:T(256)S(1)}, f32[256]{0:T(256)}, u32[]{:S(2)}) copy-start(f32[256]{0:T(256)} %param.13) | copy-start | bytes 3076
  81.5 4.5 %collective-permute-start.1 = (f32[2,32,256]{2,1,0:T(8,128)S(1)}, f32[2,32,256]{2,1,0:T(8,128)S(1)}, u32[]{:S(2)}, u32[]{:S(2)}) collective-permute-start(f32[2,32,256]{2,1,0:T(8,128)S(1)} %get-tuple-element.54), channel_id=1, source_target_pairs={{1,0},{2,1},{3,2},{4,3},{5,4},{6,5},{7,6},{9,8},{10,9},{11,10},{12... | collective-permute-start | bytes 196616 | tf_op jit(solution)/shard_map/ppermute | solution.py:22
  83.0 3.9 %collective-permute-start.2 = (f32[2,32,256]{2,1,0:T(8,128)S(1)}, f32[2,32,256]{2,1,0:T(8,128)S(1)}, u32[]{:S(2)}, u32[]{:S(2)}) collective-permute-start(f32[2,32,256]{2,1,0:T(8,128)S(1)} %get-tuple-element.53), channel_id=1, source_target_pairs={{0,1},{1,2},{2,3},{3,4},{4,5},{5,6},{6,7},{8,9},{9,10},{10,11},{11... | collective-permute-start | bytes 196616 | tf_op jit(solution)/shard_map/ppermute | solution.py:22
  87.0 4.4 %collective-permute-start.3 = (bf16[2,2,32,256]{3,2,1,0:T(8,128)(2,1)S(1)}, bf16[2,2,32,256]{3,2,1,0:T(8,128)(2,1)S(1)}, u32[]{:S(2)}, u32[]{:S(2)}) collective-permute-start(bf16[2,2,32,256]{3,2,1,0:T(8,128)(2,1)S(1)} %get-tuple-element.90), channel_id=1, source_target_pairs={{0,8},{8,16},{16,24},{1,9},{9,17},{17,25},{2,10},{10,18},{18,26},{... | collective-permute-start | bytes 196616 | tf_op jit(solution)/shard_map/ppermute | solution.py:22
  91.4 2.8 %collective-permute-start.4 = (bf16[4,1,32,256]{3,2,1,0:T(8,128)(2,1)S(1)}, bf16[4,1,32,256]{3,2,1,0:T(8,128)(2,1)S(1)}, u32[]{:S(2)}, u32[]{:S(2)}) collective-permute-start(bf16[4,1,32,256]{3,2,1,0:T(8,128)(2,1)S(1)} %get-tuple-element.88), channel_id=1, source_target_pairs={{0,1},{1,2},{2,3},{3,4},{4,5},{5,6},{6,7},{8,9},{9,10},{10,11},{11... | collective-permute-start | bytes 196616 | tf_op jit(solution)/shard_map/ppermute | solution.py:30
  92.9 5.9 %collective-permute-start.5 = (bf16[4,1,32,256]{3,2,1,0:T(8,128)(2,1)S(1)}, bf16[4,1,32,256]{3,2,1,0:T(8,128)(2,1)S(1)}, u32[]{:S(2)}, u32[]{:S(2)}) collective-permute-start(bf16[4,1,32,256]{3,2,1,0:T(8,128)(2,1)S(1)} %get-tuple-element.89), channel_id=1, source_target_pairs={{1,0},{2,1},{3,2},{4,3},{5,4},{6,5},{7,6},{9,8},{10,9},{11,10},{12... | collective-permute-start | bytes 196616 | tf_op jit(solution)/shard_map/ppermute | solution.py:33
  102.3 93.9 %all-reduce.5.cloned.1.call-start = ((), (), s32[]{:S(2)}) async-start(), calls=%async_computation.2 | async-start | bytes 884736 | tf_op jit(solution)/shard_map/psum | solution.py:109
  146.6 51.4 %copy-start.4 = (f32[256]{0:T(256)}, f32[256]{0:T(256)S(1)}, u32[]{:S(2)}) copy-start(f32[256]{0:T(256)S(1)} %get-tuple-element.97) | copy-start | bytes 3076
  146.6 51.4 %copy-start.5 = (f32[256]{0:T(256)}, f32[256]{0:T(256)S(1)}, u32[]{:S(2)}) copy-start(f32[256]{0:T(256)S(1)} %get-tuple-element.98) | copy-start | bytes 3076
Sparse Core Ops, SparseCore 0:
  102.4 47.3 reduce-scatter.1
  153.1 43.0 all-reduce.4
